TPU v7x, 256 devices: a whole 4x4x8 slice. The times are simulated.
256 devices in a mesh: bx: 16 (over z, core), by: 16 (over x, y).
Axes of the slice: x: 4, y: 4, z: 8, core: 2. Of those that a mesh axis runs over, the one named last changes fastest.
Arguments:
- density: bfloat16 [16, 16, 16, 64, 4096], P('bx', 'by'), may hold values from -5 to 5
- inner_order: int32 [16], replicated, may hold values from 0 to 15, each once
- outer_order: int32 [16], replicated, may hold values from 0 to 15, each once
- footprints: int32 [16, 16, 4], P('bx', 'by'), may hold values from 0 to 4096, as said below
Outputs:
- composite: float32 [4, 64, 4096], P(None, None, 'bx')
Inputs may be any that keep to these rules, and one draw needn't show every extreme that they name: footprints[i, j] holds first row, end row, first column and end column of brick (i, j)'s rectangle, first below end; rows lie in 0 to 64; one brick's rectangle is the whole band.
All inputs are finite; a program needn't handle non-finite values.
Results may differ from a plain program's by a relative error of at most 0.0005.
Values may be sent and summed in bfloat16 or wider, within the bound.
A program may use at most 128 MiB of HBM per device.

v0:
```python
import jax
import jax.numpy as jnp
from jax import lax
from jax.sharding import PartitionSpec as P


def palette(values):
    return jnp.stack(
        [
            jax.nn.sigmoid(2.0 * values),
            jnp.exp(-0.5 * values * values),
            jax.nn.sigmoid(-2.0 * values),
        ],
        axis=0,
    )


def advance_ray(colour, transmit, slab_data, extinct):
    for sample in range(slab_data.shape[0]):
        values = slab_data[sample].astype(jnp.float32)
        optical = extinct * values * values + 2.0 * jnp.maximum(values - 2.5, 0.0)
        survive = jnp.exp(-optical)
        colour = colour + (transmit * (1.0 - survive))[None] * palette(values)
        transmit = transmit * survive
    return (colour, transmit)


def render_slab(slab_data, extinct):
    colour = jnp.zeros((3,) + slab_data.shape[1:], jnp.float32)
    transmit = jnp.ones(slab_data.shape[1:], jnp.float32)
    colour, transmit = advance_ray(colour, transmit, slab_data, extinct)
    return jnp.concatenate([colour, (1.0 - transmit)[None]], axis=0)


def blend_over(front, behind):
    return front + (1.0 - front[3])[None] * behind


def invert_order(order):
    count = order.shape[0]
    ranks = jnp.arange(count, dtype=jnp.int32)
    return jnp.sum(ranks[:, None] * (order[:, None] == ranks[None, :]).astype(jnp.int32), axis=0)


def ordered_blend(pieces, inverse):

    def advance(rank, blended):
        chosen = lax.dynamic_index_in_dim(pieces, inverse[rank], 0, keepdims=False)
        return blend_over(blended, chosen)

    start = jnp.zeros(pieces.shape[1:], jnp.float32)
    return lax.fori_loop(0, pieces.shape[0], advance, start)


def on_device(density, inner_order, outer_order, footprints):
    across_x = lax.axis_size("bx")
    across_y = lax.axis_size("by")
    slab_data = density[0, 0]
    depth_count = slab_data.shape[0]
    extinct = 1.5 / (across_x * across_y * depth_count)
    inner_inverse = invert_order(inner_order)
    outer_inverse = invert_order(outer_order)
    bounds = footprints[0, 0]
    row_index = jnp.arange(slab_data.shape[1], dtype=jnp.int32)[:, None]
    col_index = jnp.arange(slab_data.shape[2], dtype=jnp.int32)[None, :]
    inside = (
        (row_index >= bounds[0])
        & (row_index < bounds[1])
        & (col_index >= bounds[2])
        & (col_index < bounds[3])
    )
    masked = slab_data * inside.astype(jnp.bfloat16)[None]
    image_rgba = render_slab(masked, extinct)
    received = lax.all_to_all(image_rgba[None], "bx", split_axis=3, concat_axis=0, tiled=True)
    group_image = ordered_blend(received, inner_inverse)
    gathered = lax.all_gather(group_image[None], "by", axis=0, tiled=True)
    composite = ordered_blend(gathered, outer_inverse)
    return composite


def solution(mesh):
    in_specs = (P("bx", "by", None, None, None), P(), P(), P("bx", "by", None))
    out_specs = P(None, None, "bx")
    return jax.shard_map(
        on_device, mesh=mesh, in_specs=in_specs, out_specs=out_specs, check_vma=False
    )
```

profile of v0, /device:TPU:1, one launch (start us, length us, event | category | flops | bytes accessed | tf_op | source)
XLA Modules:
  0.0 403.5 jit_solution(12214206967363046123)
XLA Ops:
  6.5 1.5 fusion.260
  8.0 1.4 iota_compare_fusion
  9.4 1.2 compare_and_fusion
  10.8 7.5 %bitcast_multiply_fusion.2 = bf16[16,64,4096]{2,1,0:T(8,128)(2,1)} fusion(bf16[1,1,16,64,4096]{4,3,2,1,0:T(8,128)(2,1)} %param.8, bf16[64,4096]{1,0:T(8,128)(2,1)S(1)} %and_convert_fusion), kind=kLoop, calls=%fused_computation.10 | loop fusion | flops 4194304 | bytes 17301504 | tf_op jit(solution)/shard_map/mul | solution.py:72
  18.3 4.9 %multiply_bitcast_fusion.11 = (f32[64,4096]{1,0:T(8,128)}, f32[1,64,4096]{2,1,0:T(8,128)}) fusion(bf16[16,64,4096]{2,1,0:T(8,128)(2,1)} %bitcast_multiply_fusion.2), kind=kLoop, calls=%fused_computation.391 | loop fusion | flops 11796480 | bytes 4718592 | tf_op jit(solution)/shard_map/mul | solution.py:23
  23.2 6.0 %subtract_bitcast_fusion = (f32[64,4096]{1,0:T(8,128)S(1)}, f32[1,64,4096]{2,1,0:T(8,128)S(1)}, f32[1,64,4096]{2,1,0:T(8,128)S(1)}, f32[1,64,4096]{2,1,0:T(8,128...) fusion(bf16[16,64,4096]{2,1,0:T(8,128)(2,1)} %bitcast_multiply_, ...), kind=kLoop, calls=%fused_computation.395 | loop fusion | flops 19398656 | bytes 24117248 | tf_op jit(solution)/shard_map/mul | solution.py:23
  29.2 6.5 %multiply_bitcast_fusion.14 = (f32[64,4096]{1,0:T(8,128)S(1)}, f32[1,64,4096]{2,1,0:T(8,128)S(1)}, f32[1,64,4096]{2,1,0:T(8,128)S(1)}, f32[1,64,4096]{2,1,0:T(8,...) fusion(bf16[16,64,4096]{2,1,0:T(8,128)(2,1)S(1)} %bitcast.74), kind=kLoop, calls=%fused_computation.394 | loop fusion | flops 21233664 | bytes 23592960 | tf_op jit(solution)/shard_map/mul | solution.py:23
  35.7 6.1 %multiply_bitcast_fusion.13 = (f32[64,4096]{1,0:T(8,128)}, f32[1,64,4096]{2,1,0:T(8,128)}, f32[1,64,4096]{2,1,0:T(8,128)}, f32[1,64,4096]{2,1,0:T(8,128)}, f32[1...) fusion(bf16[16,64,4096]{2,1,0:T(8,128)(2,1)S(1)} %bitcast.74), kind=kLoop, calls=%fused_computation.393 | loop fusion | flops 20185088 | bytes 18350080 | tf_op jit(solution)/shard_map/mul | solution.py:23
  41.8 3.2 multiply_bitcast_fusion.7
  45.0 3.2 multiply_bitcast_fusion.3
  48.1 4.1 %multiply_bitcast_fusion.2 = (f32[64,4096]{1,0:T(8,128)}, f32[1,64,4096]{2,1,0:T(8,128)}, f32[64,4096]{1,0:T(8,128)}, f32[64,4096]{1,0:T(8,128)}, f32[64,4096]{1,0:T(8,128)}) fusion(bf16[16,64,4096]{2,1,0:T(8,128)(2,1)S(1)} %bitcast.74, f32[1,64,4096]{2,1,0:T(8,128)S(1)} %get-tuple-element.236), kind=kLoop, calls=%fused_computation.382 | loop fusion | flops 20709376 | bytes 10485760 | tf_op jit(solution)/shard_map/mul | solution.py:23
  52.3 14.6 %fusion.18 = f32[3,64,4096]{2,1,0:T(8,128)S(1)} fusion(f32[1,64,4096]{2,1,0:T(8,128)} %get-tuple-element.290, f32[1,64,4096]{2,1,0:T(8,128)S(1)} %get-tuple-element.252, f32[1,64,4096]{2,1,0:T(8,128)S(1)} %get-tuple-element.260, f32[1,64,4096]{2,1,0:T(8,128)} %get-tuple-element.269, f32[1,64,4096]{2,1,0:T(8,128)} %get-tuple-element.277, ...), kind=kLoop, calls=%fused_computation.27 | loop fusion | flops 49545216 | bytes 70254592 | tf_op jit(solution)/shard_map/add | solution.py:23
  66.9 2.3 maximum_bitcast_fusion
  69.2 8.4 %copy.95 = f32[1,4,64,4096]{2,1,0,3:T(4,128)} copy(f32[1,4,64,4096]{3,2,1,0:T(8,128)} %maximum_bitcast_fusion) | data formatting | bytes 8388608 | tf_op jit(solution)/shard_map/broadcast_in_dim | solution.py:74
  77.6 14.6 %reshape.75 = f32[16,1,65536]{2,1,0:T(1,128)} reshape(f32[4096,1,4,64]{3,2,1,0:T(4,128)} %bitcast.75) | data formatting | bytes 8388608
  92.1 10.1 %all-to-all-start = ((f32[16,1,65536]{2,1,0:T(1,128)}), f32[16,1,65536]{2,1,0:T(1,128)}, u32[]{:S(2)}, u32[]{:S(2)}) async-start(f32[16,1,65536]{2,1,0:T(1,128)} %reshape.75), calls=%async_computation | async-start | bytes 8388608 | tf_op jit(solution)/shard_map/all_to_all | solution.py:74
  102.6 93.2 %all-to-all-done = f32[16,1,65536]{2,1,0:T(1,128)} async-done(((f32[16,1,65536]{2,1,0:T(1,128)}), f32[16,1,65536]{2,1,0:T(1,128)}, u32[]{:S(2)}, u32[]{:S(2)}) %all-to-all-start) | async-done | bytes 4194336 | tf_op jit(solution)/shard_map/all_to_all | solution.py:74
  196.4 13.7 %reduce = f32[16,65536]{1,0:T(8,128)} reduce(f32[16,1,65536]{2,1,0:T(1,128)} %all-to-all-done, f32[]{:T(128)} %broadcast.1324), dimensions={1}, to_apply=%all_to_all.13.reduce_sub_computation | reduce | bytes 8388612 | tf_op jit(solution)/shard_map/all_to_all | solution.py:74
  210.1 9.3 %reshape.76 = f32[4096,1,4,64]{3,2,1,0:T(4,128)} reshape(f32[16,65536]{1,0:T(8,128)} %reduce) | data formatting | bytes 8388608
  219.4 8.5 %copy.99 = f32[1,4,64,16,256]{4,2,1,3,0:T(8,128)} copy(f32[1,4,64,16,256]{2,1,4,3,0:T(4,128)} %bitcast.76) | data formatting | bytes 8388608 | tf_op jit(solution)/shard_map/all_to_all | solution.py:74
  227.9 53.0 %while.28 = (s32[]{:T(128)}, f32[4,64,256]{2,1,0:T(8,128)S(1)}, s32[16]{0:T(128)S(1)}, f32[16,4,64,256]{3,2,1,0:T(8,128)}, s32[]{:T(128)}, /*index=5*/s32[]{:T(128)}, s32[]{:T(128)}) while((s32[]{:T(128)}, f32[4,64,256]{2,1,0:T(8,128)S(1)}, s32[16]{0:T(128)S(1)}, f32[16,4,64,256]{3,2,1,0:T(8,128)}, s32[]{:T(128)}, ...), condition=%wide.region_3.4_spmd.clone, body=%wide.region_2.3_spmd.clone.sunk | while | flops 278534 | bytes 1507466 | solution.py:52
  236.8 1.0 fusion.266
  281.7 55.9 %all-gather.3.cloned.1.call-done = f32[64,64,256]{2,1,0:T(8,128)} async-done(((f32[4,64,256]{2,1,0:T(8,128)}), f32[64,64,256]{2,1,0:T(8,128)}) %all-gather.3.cloned.1.call-update) | async-done | bytes 4194320 | tf_op jit(solution)/shard_map/all_gather | solution.py:76
  337.7 58.3 %while.29 = (s32[]{:T(128)}, f32[4,64,256]{2,1,0:T(8,128)S(1)}, s32[16]{0:T(128)S(1)}, f32[16,4,64,256]{3,2,1,0:T(8,128)}, s32[]{:T(128)}, /*index=5*/s32[]{:T(128)}, s32[]{:T(128)}) while((s32[]{:T(128)}, f32[4,64,256]{2,1,0:T(8,128)S(1)}, s32[16]{0:T(128)S(1)}, f32[16,4,64,256]{3,2,1,0:T(8,128)}, s32[]{:T(128)}, ...), condition=%wide.region_5.6_spmd.clone, body=%wide.region_4.5_spmd.clone.sunk | while | flops 278534 | bytes 1507466 | solution.py:52
  (152 shorter events, 54.3 us)
Async XLA Ops:
  18.3 10.9 %slice-start = ((s8[8388608]{0:T(1024)(128)(4,1)}), s8[4194304]{0:T(1024)(128)(4,1)S(1)}, s32[]{:S(2)}) async-start(s8[8388608]{0:T(1024)(128)(4,1)} %bitcast.73), calls=%async_computation.2 | async-start | bytes 8388608
  23.2 6.1 %slice-start.1 = ((s8[8388608]{0:T(1024)(128)(4,1)}), s8[4194304]{0:T(1024)(128)(4,1)S(1)}, s32[]{:S(2)}) async-start(s8[8388608]{0:T(1024)(128)(4,1)} %bitcast.73), calls=%async_computation.3 | async-start | bytes 8388608
  35.7 6.1 %copy-start.2 = (f32[1,64,4096]{2,1,0:T(8,128)S(1)}, f32[1,64,4096]{2,1,0:T(8,128)}, u32[]{:S(2)}) copy-start(f32[1,64,4096]{2,1,0:T(8,128)} %get-tuple-element.232) | copy-start | bytes 3145732
  52.3 14.6 %copy-start.3 = (f32[1,64,4096]{2,1,0:T(8,128)S(1)}, f32[1,64,4096]{2,1,0:T(8,128)}, u32[]{:S(2)}) copy-start(f32[1,64,4096]{2,1,0:T(8,128)} %get-tuple-element.244) | copy-start | bytes 3145732
  92.1 10.4 %copy-start.4 = (s32[16]{0:T(128)S(1)}, s32[16]{0:T(128)}, u32[]{:S(2)}) copy-start(s32[16]{0:T(128)} %param.9) | copy-start | bytes 196
  92.1 103.7 %all-to-all-start = ((f32[16,1,65536]{2,1,0:T(1,128)}), f32[16,1,65536]{2,1,0:T(1,128)}, u32[]{:S(2)}, u32[]{:S(2)}) async-start(f32[16,1,65536]{2,1,0:T(1,128)} %reshape.75), calls=%async_computation | async-start | bytes 8388608 | tf_op jit(solution)/shard_map/all_to_all | solution.py:74
  102.2 235.4 %all-gather.3.cloned.1.call-start = ((), (), s32[]{:S(2)}) async-start(), calls=%async_computation.1 | async-start | bytes 4456448 | tf_op jit(solution)/shard_map/all_gather | solution.py:76
  227.9 53.7 %copy-start.5 = (s32[16]{0:T(128)S(1)}, s32[16]{0:T(128)}, u32[]{:S(2)}) copy-start(s32[16]{0:T(128)} %param.10) | copy-start | bytes 196
  280.9 0.7 copy-start
  396.0 0.7 copy-start.1
Sparse Core Ops, SparseCore 0:
  281.7 55.8 all-gather.2
where the time goes:
time: 406 us; the launch traced here: 404 us
  waiting for transfers between devices  149 us (37%)
  other arithmetic  109 us (27%)
  local copies, waits for them, and re-layouts  62.5 us (15%)
  loops' own time  58.6 us (14%)
  between operations  13.6 us (3%)
  starting transfers between devices  10.4 us (3%)
    all_to_all x1, waiting for transfers between devices, on_device(): lax.all_to_all(image_rgba[None], 'bx', split_axis=3, concat_axis=0, tiled...  93.2 us
    another operation x2, loops' own time, ordered_blend(): return lax.fori_loop(0, pieces.shape[0], advance, start)  58.6 us
    all_gather x1, waiting for transfers between devices, on_device(): gathered = lax.all_gather(group_image[None], 'by', axis=0, tiled=True)  55.9 us
    mul x7, other arithmetic, advance_ray(): colour = colour + (transmit * (1.0 - survive))[None] * palette(values)  34 us
    add x32, other arithmetic, blend_over(): return front + (1.0 - front[3])[None] * behind  33.5 us
    unnamed x18, local copies, waits for them, and re-layouts  25.3 us
    dynamic_slice x32, local copies, waits for them, and re-layouts, advance(): chosen = lax.dynamic_index_in_dim(pieces, inverse[rank], 0, keepdims=False)  18.3 us
    add x1, other arithmetic, advance_ray(): colour = colour + (transmit * (1.0 - survive))[None] * palette(values)  14.6 us
  transfers between devices with their start and end apart: 2, of which 2 were waited for; matrix products, arithmetic and copies ran while one was open for 0% of the time, Pallas kernels for 0%

commit v1 on v0

v1 whole, which is shorter than its diff:
```python
import functools

import jax
import jax.numpy as jnp
from jax import lax
from jax.experimental import pallas as pl
from jax.experimental.pallas import tpu as pltpu
from jax.sharding import PartitionSpec as P

MESH = pl.DeviceIdType.MESH
LOG2E = 1.4426950408889634
TILE_ROWS = 16
WIDTH = 256
FIRST = 2
CODE = 65534.0


def encode(value):
    root = lax.rsqrt(lax.rsqrt(jnp.maximum(value, 0.0)))
    return (root * CODE + 0.5).astype(jnp.int32).astype(jnp.uint16)


def decode(code):
    root = code.astype(jnp.int32).astype(jnp.float32)
    square = root * root * (1.0 / (CODE * CODE))
    return square * square


def march(load, depth, extinct):
    transmit = tanhs = green = None
    for sample in range(depth):
        values = load(sample).astype(jnp.float32)
        square = values * values
        bend = jnp.minimum((2.5 - values) * (2.0 * LOG2E), 0.0)
        survive = jnp.exp2(square * (-extinct * LOG2E) + bend)
        bell = jnp.exp2(square * (-0.5 * LOG2E))
        slope = jnp.tanh(values)
        if sample == 0:
            left = survive
            weight = 1.0 - survive
            tanhs = weight * slope
            green = weight * bell
        else:
            left = transmit * survive
            weight = transmit - left
            tanhs = tanhs + weight * slope
            green = green + weight * bell
        transmit = left
    opaque = 1.0 - transmit
    return 0.5 * (opaque + tanhs), green, 0.5 * (opaque - tanhs)


def blend(images, order_ref, count):
    red = green = blue = through = None
    for rank in range(count):
        at = order_ref[rank]
        r, g, b = images[at, 0], images[at, 1], images[at, 2]
        clear = 1.0 - (r + b)
        if rank == 0:
            red, green, blue, through = r, g, b, clear
        else:
            red = red + through * r
            green = green + through * g
            blue = blue + through * b
            through = through * clear
    return red, green, blue


def kernel(
    sizes,
    extinct,
    inner_hbm,
    outer_hbm,
    bounds_hbm,
    density_ref,
    out_ref,
    slab,
    sending,
    landed,
    groups,
    images,
    inner_ref,
    outer_ref,
    bounds_ref,
    inner_inverse,
    outer_inverse,
    small_sem,
    load_sem,
    send_sem,
    recv_sem,
    group_send_sem,
    group_recv_sem,
):
    across_x, across_y, side, depth, rows, columns = sizes
    chips = across_x // 2
    block = columns // across_x
    halves = block // WIDTH
    pieces = rows // TILE_ROWS * halves
    strips = rows // TILE_ROWS
    i = lax.axis_index("bx")
    j = lax.axis_index("by")
    z, core = i // 2, i % 2
    x, y = j // side, j % side

    def column_peer(n):
        step = n // 2
        hops = chips // 2 + (1 - 2 * (step % 2)) * ((step + 1) // 2)
        return (z + hops) % chips * 2 + (core + 1 - n % 2) % 2

    def group_peer(n):
        return (x + n // side) % side * side + (y + n % side) % side

    def load(strip):
        return pltpu.make_async_copy(
            density_ref.at[0, 0, :, pl.ds(pl.multiple_of(strip * TILE_ROWS, TILE_ROWS), TILE_ROWS), :],
            slab.at[strip],
            load_sem.at[strip],
        )

    def column_copy(piece, n):
        return pltpu.make_async_remote_copy(
            src_ref=sending.at[piece, n],
            dst_ref=landed.at[piece, i],
            send_sem=send_sem.at[piece, n],
            recv_sem=recv_sem.at[piece, i],
            device_id=(column_peer(n), j),
            device_id_type=MESH,
        )

    def column_arrival(piece, n):
        peer = column_peer(n)
        return pltpu.make_async_remote_copy(
            src_ref=sending.at[piece, n],
            dst_ref=landed.at[piece, peer],
            send_sem=send_sem.at[piece, n],
            recv_sem=recv_sem.at[piece, peer],
            device_id=(peer, j),
            device_id_type=MESH,
        )

    def group_copy(piece, n):
        return pltpu.make_async_remote_copy(
            src_ref=groups.at[piece, j],
            dst_ref=groups.at[piece, j],
            send_sem=group_send_sem.at[piece, n],
            recv_sem=group_recv_sem.at[piece, j],
            device_id=(i, group_peer(n)),
            device_id_type=MESH,
        )

    def group_arrival(piece, n):
        peer = group_peer(n)
        return pltpu.make_async_remote_copy(
            src_ref=groups.at[piece, j],
            dst_ref=groups.at[piece, peer],
            send_sem=group_send_sem.at[piece, n],
            recv_sem=group_recv_sem.at[piece, peer],
            device_id=(i, peer),
            device_id_type=MESH,
        )

    def each(count, act, first=0):
        def step(n, carry):
            act(n)
            return carry

        lax.fori_loop(first, count, step, 0)

    def render(piece, n, store):
        strip = piece // halves
        left = pl.multiple_of(column_peer(n) * block + piece % halves * WIDTH, WIDTH)
        colours = march(lambda s: slab[strip, s, :, pl.ds(left, WIDTH)], depth, extinct)
        row = lax.broadcasted_iota(jnp.int32, (TILE_ROWS, WIDTH), 0) + strip * TILE_ROWS
        column = lax.broadcasted_iota(jnp.int32, (TILE_ROWS, WIDTH), 1) + left
        inside = (
            (row >= bounds_ref[0, 0, 0])
            & (row < bounds_ref[0, 0, 1])
            & (column >= bounds_ref[0, 0, 2])
            & (column < bounds_ref[0, 0, 3])
        )
        for channel, colour in enumerate(colours):
            store(channel, encode(jnp.where(inside, colour, 0.0)))

    def render_send(piece, n):
        def store(channel, codes):
            sending[piece, n, channel] = codes

        render(piece, n, store)

    def render_keep(piece):
        def keep(channel, codes):
            landed[piece, i, channel] = codes

        render(piece, across_x - 1, keep)

    def take(buffer, piece, at):
        codes = buffer[piece, at]
        for channel in range(3):
            images[at, channel] = decode(codes[channel])

    def finish(piece):
        take(groups, piece, j)

        def arrive(n):
            group_arrival(piece, n).wait_recv()
            take(groups, piece, group_peer(n))

        each(across_y, arrive, 1)
        red, green, blue = blend(images, outer_inverse, across_y)
        top = pl.multiple_of(piece // halves * TILE_ROWS, TILE_ROWS)
        left = pl.multiple_of(piece % halves * WIDTH, WIDTH)
        where = (pl.ds(top, TILE_ROWS), pl.ds(left, WIDTH))
        out_ref[(0,) + where] = red
        out_ref[(1,) + where] = green
        out_ref[(2,) + where] = blue
        out_ref[(3,) + where] = red + blue

    small = [
        pltpu.make_async_copy(inner_hbm, inner_ref, small_sem.at[0]),
        pltpu.make_async_copy(outer_hbm, outer_ref, small_sem.at[1]),
        pltpu.make_async_copy(bounds_hbm, bounds_ref, small_sem.at[2]),
    ]
    small[2].start()
    each(strips, lambda strip: load(strip).start())
    small[0].start()
    small[1].start()

    barrier = pltpu.get_barrier_semaphore()

    def greet_column(n):
        pl.semaphore_signal(barrier, inc=1, device_id=(column_peer(n), j), device_id_type=MESH)

    def greet_group(n):
        pl.semaphore_signal(barrier, inc=1, device_id=(i, group_peer(n)), device_id_type=MESH)

    each(across_x - 1, greet_column)
    each(across_y, greet_group, 1)

    small[2].wait()
    load(0).wait()
    each(FIRST, lambda n: render_send(0, n))
    pl.semaphore_wait(barrier, across_x - 1 + across_y - 1)
    each(FIRST, lambda n: column_copy(0, n).start())

    def render_and_send(piece, n):
        render_send(piece, n)
        column_copy(piece, n).start()

    each(across_x - 1, lambda n: render_and_send(0, n), FIRST)
    render_keep(0)

    def follow(piece):
        @pl.when(piece % halves == 0)
        def _():
            load(piece // halves).wait()

        each(across_x - 1, lambda n: render_and_send(piece, n))
        render_keep(piece)

    each(pieces, follow, 1)

    def invert(order_ref, inverse_ref, count):
        def one(rank):
            found = jnp.int32(0)
            for at in range(count):
                found = jnp.where(order_ref[at] == rank, at, found)
            inverse_ref[rank] = found

        each(count, one)

    small[0].wait()
    small[1].wait()
    invert(inner_ref, inner_inverse, across_x)
    invert(outer_ref, outer_inverse, across_y)

    def advance(piece):
        take(landed, piece, i)

        def arrive(n):
            column_arrival(piece, n).wait_recv()
            take(landed, piece, column_peer(n))

        each(across_x - 1, arrive)
        red, green, blue = blend(images, inner_inverse, across_x)
        groups[piece, j, 0] = encode(red)
        groups[piece, j, 1] = encode(green)
        groups[piece, j, 2] = encode(blue)
        each(across_y, lambda n: group_copy(piece, n).start(), 1)

        @pl.when(piece >= 1)
        def _():
            finish(piece - 1)

    each(pieces, advance)
    finish(pieces - 1)

    def drain(piece):
        each(across_x - 1, lambda n: column_copy(piece, n).wait_send())
        each(across_y, lambda n: group_copy(piece, n).wait_send(), 1)

    each(pieces, drain)


def on_device(density, inner_order, outer_order, footprints):
    across_x = lax.axis_size("bx")
    across_y = lax.axis_size("by")
    depth, rows, columns = density.shape[2:]
    extinct = 1.5 / (across_x * across_y * depth)
    side = 1
    while side * side < across_y:
        side *= 2
    block = columns // across_x
    pieces = rows // TILE_ROWS * (block // WIDTH)
    strips = rows // TILE_ROWS
    piece_shape = (3, TILE_ROWS, WIDTH)
    hbm = pl.BlockSpec(memory_space=pltpu.HBM)
    return pl.pallas_call(
        functools.partial(kernel, (across_x, across_y, side, depth, rows, columns), extinct),
        out_shape=jax.ShapeDtypeStruct((4, rows, block), jnp.float32),
        in_specs=[hbm] * 4,
        out_specs=pl.BlockSpec(memory_space=pltpu.VMEM),
        scratch_shapes=[
            pltpu.VMEM((strips, depth, TILE_ROWS, columns), jnp.bfloat16),
            pltpu.VMEM((pieces, across_x - 1) + piece_shape, jnp.uint16),
            pltpu.VMEM((pieces, across_x) + piece_shape, jnp.uint16),
            pltpu.VMEM((pieces, across_y) + piece_shape, jnp.uint16),
            pltpu.VMEM((max(across_x, across_y),) + piece_shape, jnp.float32),
            pltpu.SMEM((across_x,), jnp.int32),
            pltpu.SMEM((across_y,), jnp.int32),
            pltpu.SMEM((1, 1, 4), jnp.int32),
            pltpu.SMEM((across_x,), jnp.int32),
            pltpu.SMEM((across_y,), jnp.int32),
            pltpu.SemaphoreType.DMA((3,)),
            pltpu.SemaphoreType.DMA((strips,)),
            pltpu.SemaphoreType.DMA((pieces, across_x)),
            pltpu.SemaphoreType.DMA((pieces, across_x)),
            pltpu.SemaphoreType.DMA((pieces, across_y)),
            pltpu.SemaphoreType.DMA((pieces, across_y)),
        ],
        compiler_params=pltpu.CompilerParams(
            collective_id=0, has_side_effects=True, vmem_limit_bytes=60 << 20
        ),
    )(inner_order, outer_order, footprints, density)


def solution(mesh):
    in_specs = (P("bx", "by", None, None, None), P(), P(), P("bx", "by", None))
    out_specs = P(None, None, "bx")
    return jax.shard_map(
        on_device, mesh=mesh, in_specs=in_specs, out_specs=out_specs, check_vma=False
    )
```

time: 406 us -> 59.5 us (0.15)
  waiting for transfers between devices: 149 us -> 0 us
  other arithmetic: 109 us -> 0 us
  local copies, waits for them, and re-layouts: 62.5 us -> 1.67 us
  loops' own time: 58.6 us -> 0 us
  Pallas kernels: 0 us -> 57.7 us
  between operations: 13.6 us -> 0.01 us
  starting transfers between devices: 10.4 us -> 0 us
    all_to_all x1 -> x0, waiting for transfers between devices: 93.2 us -> none  [on_device(): lax.all_to_all(image_rgba[None], 'bx', split_axis=3, concat_axis=0, tiled...]
    another operation x2 -> x0, loops' own time: 58.6 us -> none  [ordered_blend(): return lax.fori_loop(0, pieces.shape[0], advance, start)]
    pallas_call x0 -> x1, Pallas kernels: none -> 57.7 us  [on_device(): pl.pallas_call(functools.partial(kernel, (across_x, across_y, side, depth...]
    all_gather x1 -> x0, waiting for transfers between devices: 55.9 us -> none  [on_device(): gathered = lax.all_gather(group_image[None], 'by', axis=0, tiled=True)]
    add x33 -> x0, other arithmetic: 48.1 us -> none  [the longest x32 33.5 us: blend_over(): return front + (1.0 - front[3])[None] * behind]
    mul x40 -> x0, other arithmetic: 41.7 us -> none  [the longest x7 34 us: advance_ray(): colour = colour + (transmit * (1.0 - survive))[None] * palette(values)]
    unnamed x18 -> x1, local copies, waits for them, and re-layouts: 25.3 us -> 1.67 us
    dynamic_slice x32 -> x0, local copies, waits for them, and re-layouts: 18.3 us -> none  [advance(): chosen = lax.dynamic_index_in_dim(pieces, inverse[rank], 0, keepdims=False)]
  transfers between devices with their start and end apart: 2 -> 0, of which waited for: 2 -> 0; matrix products, arithmetic and copies ran while one was open for 0% -> 0% of each run, Pallas kernels for 0% -> 0%
where the time goes in v1:
time: 59.5 us; the launch traced here: 59.4 us
  Pallas kernels  57.7 us (97%)
  local copies, waits for them, and re-layouts  1.67 us (3%)
    pallas_call x1, Pallas kernels, on_device(): pl.pallas_call(functools.partial(kernel, (across_x, across_y, side, depth...  57.7 us
    unnamed x1, local copies, waits for them, and re-layouts  1.67 us

profile of v1, /device:TPU:1, one launch (start us, length us, event | category | flops | bytes accessed | tf_op | source)
XLA Modules:
  0.0 59.4 jit_solution(9426701951246352810)
XLA Ops:
  0.0 57.7 %shard_map.46 = f32[4,64,256]{2,1,0:T(8,128)} custom-call(s32[16]{0:T(128)} %inner_hbm.1, s32[16]{0:T(128)} %outer_hbm.1, s32[1,1,4]{2,1,0:T(1,128)} %bounds_hbm.1, bf16[1,1,16,64,4096]{4,3,2,1,0:T(8,128)(2,1)} %density_ref.1), custom_call_target="tpu_custom_call" | custom-call | tf_op jit(solution)/shard_map/pallas_call | solution.py:317
  57.7 1.7 %copy.6 = f32[4,64,256]{2,1,0:T(8,128)} copy(f32[4,64,256]{2,1,0:T(8,128)} %shard_map.46) | data formatting | bytes 524288
